TPU v7x, 512 devices: a whole 4x4x16 slice. The times are simulated.
512 devices in a mesh: layer: 8 (over z_hi, x), row: 8 (over z_lo), col: 8 (over y, core).
Axes of the slice: x: 4, y: 4, z: 16 (z_hi: 2, z_lo: 8; z = z_hi * 8 + z_lo), core: 2. Of those that a mesh axis runs over, the one named last changes fastest.
Arguments:
- covariance: float32 [65536, 8192], P(('layer', 'row'), 'col'), parts along dimension 0, may hold values from -2 to 20, as said below
- weight: bfloat16 [65536, 2, 1024], P(('layer', 'col', 'row')), parts along dimension 0, may hold values from -6 to 6
- factor_a: bfloat16 [65536, 2, 256], P(('layer', 'col', 'row')), parts along dimension 0, may hold values from -1.5 to 1.5
- factor_b: bfloat16 [16, 256, 1024], P('layer', ('row', 'col')), parts along dimension 0, may hold values from -1.5 to 1.5
Outputs:
- new_a: float32 [65536, 2, 256], P(('layer', 'col', 'row')), parts along dimension 0
- new_b: float32 [16, 256, 1024], P('layer', ('row', 'col')), parts along dimension 0
There are 8 independent parts, one for each index of `layer`. A program takes and returns all parts, laid end to end along the dimension named above; each array names one. Nothing has to cross between parts.
Inputs may be any that keep to these rules, and one draw needn't show every extreme that they name: covariance is symmetric and positive definite.
All inputs are finite; a program needn't handle non-finite values.
Results may differ from a plain program's by a relative error of at most 0.0012.
Values may be sent and summed in bfloat16 or wider, within the bound.
A program may use at most 64 MiB of HBM per device.

v0:
```python
import jax
import jax.numpy as jnp
from jax import lax
from jax.sharding import PartitionSpec as P

D = 8192
O = 1024
R = 256


def reorder_slots(spread):
    side = lax.axis_size("row")
    total = side * side
    return spread.reshape(side, side, -1).transpose(1, 0, 2).reshape(total, -1)


def transpose_full(values):
    side = lax.axis_size("row")
    flat = values.reshape(side * side, -1)
    spread = lax.all_to_all(flat, ("row", "col"), split_axis=0, concat_axis=0, tiled=True)
    landed = lax.all_to_all(
        reorder_slots(spread), ("row", "col"), split_axis=0, concat_axis=0, tiled=True
    )
    return landed.reshape(values.shape)


def per_device(covariance, weight, factor_a, factor_b):
    highest = lax.Precision.HIGHEST
    row_count = weight.shape[0]
    full_b = lax.all_gather(factor_b, ("row", "col"), axis=1, tiled=True)
    right_f = full_b.astype(jnp.float32)
    diff_one = (
        weight.astype(jnp.float32)
        - jnp.einsum("nkr,kro->nko", factor_a, full_b, preferred_element_type=jnp.float32)
    ).astype(jnp.bfloat16)
    panels = jnp.einsum(
        "nko,kro->nkr",
        lax.all_gather(diff_one, "row", axis=0, tiled=True),
        full_b,
        preferred_element_type=jnp.float32,
    )
    panel_flat = panels.reshape(panels.shape[0], -1)
    cov_rows = covariance
    grad_one = lax.psum_scatter(
        jnp.dot(cov_rows, panel_flat, precision=highest, preferred_element_type=jnp.float32),
        "col",
        scatter_dimension=0,
        tiled=True,
    )
    grad_one = transpose_full(grad_one)
    new_a = factor_a.astype(jnp.float32) + 4.0 / O * grad_one.reshape(row_count, 2, R)
    diff_two = (
        weight.astype(jnp.float32) - jnp.einsum("nkr,kro->nko", new_a, right_f, precision=highest)
    ).astype(jnp.bfloat16)
    a_panel = lax.all_gather(new_a.reshape(row_count, 2 * R), "row", axis=0, tiled=True)
    cov_rows = covariance
    field = lax.psum_scatter(
        jnp.dot(cov_rows, a_panel, precision=highest, preferred_element_type=jnp.float32),
        "col",
        scatter_dimension=0,
        tiled=True,
    )
    field = transpose_full(field)
    partial_value = jnp.einsum(
        "nkr,nko->kro",
        field.reshape(row_count, 2, R),
        diff_two.astype(jnp.float32),
        precision=highest,
    )
    summed = lax.psum(partial_value, ("row", "col"))
    share_rows = factor_b.shape[1]
    linear_id = lax.axis_index("row") * lax.axis_size("col") + lax.axis_index("col")
    own_share = lax.dynamic_slice_in_dim(summed, linear_id * share_rows, share_rows, 1)
    new_b = factor_b.astype(jnp.float32) + 8.0 / D * own_share
    return (new_a, new_b)


def solution(mesh):
    in_specs = (
        P(("layer", "row"), "col"),
        P(("layer", "col", "row"), None, None),
        P(("layer", "col", "row"), None, None),
        P("layer", ("row", "col"), None),
    )
    out_specs = (P(("layer", "col", "row"), None, None), P("layer", ("row", "col"), None))
    return jax.shard_map(
        per_device, mesh=mesh, in_specs=in_specs, out_specs=out_specs, check_vma=False
    )
```

profile of v0, /device:TPU:1, one launch (start us, length us, event | category | flops | bytes accessed | tf_op | source)
XLA Modules:
  0.0 1366.5 jit_solution(1264701732032202692)
XLA Ops:
  7.2 1.3 copy.42
  8.6 1.4 copy.41
  10.0 125.7 %all-gather.4.cloned.1.call-done = bf16[2,256,1024]{2,0,1:T(2,128)(2,1)} async-done(((bf16[2,4,1024]{2,0,1:T(2,128)(2,1)}), bf16[2,256,1024]{2,0,1:T(2,128)(2,1)}) %all-gather.4.cloned.1.call-update) | async-done | bytes 1048592 | tf_op jit(solution)/shard_map/all_gather | solution.py:30
  135.7 2.7 fusion.3
  138.5 101.9 %all-gather.6.cloned.1.call-done = bf16[1024,2,1024]{0,2,1:T(8,128)(2,1)} async-done(((bf16[128,2,1024]{0,2,1:T(8,128)(2,1)}), bf16[1024,2,1024]{0,2,1:T(8,128)(2,1)}) %all-gather.6.cloned.1.call-update) | async-done | bytes 4194320 | tf_op jit(solution)/shard_map/all_gather | solution.py:38
  240.4 3.6 fusion.5
  244.0 8.3 convolution_bitcast_fusion.1
  252.3 39.2 %reduce-scatter.3.cloned.1.call-done = f32[128,512]{0,1:T(8,128)} async-done(((f32[1024,512]{0,1:T(8,128)}), f32[128,512]{0,1:T(8,128)}) %reduce-scatter.3.cloned.1.call-update) | async-done | bytes 262160 | tf_op jit(solution)/shard_map/reduce_scatter | solution.py:44
  291.5 1.1 copy.47
  292.9 32.7 %all_to_all.38 = f32[64,1,1024]{2,1,0:T(1,128)S(1)} all-to-all(f32[64,1,1024]{2,1,0:T(1,128)S(1)} %all_to_all.32), channel_id=1, replica_groups=mesh['layer'=8,'row'=8,'col'=8] {'row','col'}, dimensions={0} | all-to-all | bytes 524288 | tf_op jit(solution)/shard_map/all_to_all | solution.py:20
  326.1 25.6 %all_to_all.39 = f32[64,1,1024]{2,1,0:T(1,128)S(1)} all-to-all(f32[64,1,1024]{2,1,0:T(1,128)S(1)} %copy.50), channel_id=1, replica_groups=mesh['layer'=8,'row'=8,'col'=8] {'row','col'}, dimensions={0} | all-to-all | bytes 524288 | tf_op jit(solution)/shard_map/all_to_all | solution.py:21
  352.7 0.8 copy.65
  353.6 58.1 %all-gather.8.cloned.1.call-done = f32[1024,512]{1,0:T(8,128)} async-done(((f32[128,512]{1,0:T(8,128)}), f32[1024,512]{1,0:T(8,128)}) %all-gather.8.cloned.1.call-update) | async-done | bytes 2097168 | tf_op jit(solution)/shard_map/all_gather | solution.py:55
  411.7 16.7 %convolution_bitcast_fusion = f32[1024,512]{0,1:T(8,128)} fusion(f32[1024,512]{1,0:T(8,128)} %all-gather.8.cloned.1.call-done, f32[1024,1024]{1,0:T(8,128)} %param.4), kind=kOutput, calls=%fused_computation | convolution fusion | flops 6442450944 | bytes 8388608 | tf_op jit(solution)/shard_map/dot_general | solution.py:58
  428.4 40.4 %reduce-scatter.5.cloned.1.call-done = f32[128,512]{0,1:T(8,128)} async-done(((f32[1024,512]{0,1:T(8,128)}), f32[128,512]{0,1:T(8,128)}) %reduce-scatter.5.cloned.1.call-update) | async-done | bytes 262160 | tf_op jit(solution)/shard_map/reduce_scatter | solution.py:57
  468.8 1.1 copy.51
  470.2 32.8 %all_to_all.40 = f32[64,1,1024]{2,1,0:T(1,128)S(1)} all-to-all(f32[64,1,1024]{2,1,0:T(1,128)S(1)} %all_to_all.33), channel_id=1, replica_groups=mesh['layer'=8,'row'=8,'col'=8] {'row','col'}, dimensions={0} | all-to-all | bytes 524288 | tf_op jit(solution)/shard_map/all_to_all | solution.py:20
  503.2 1.0 copy.54
  504.2 5.9 all-to-all-start.3
  510.4 1.3 fusion.2
  511.8 18.2 %all-to-all-done.3 = f32[64,1,1024]{2,1,0:T(1,128)S(1)} async-done(((f32[64,1,1024]{2,1,0:T(1,128)}), f32[64,1,1024]{2,1,0:T(1,128)S(1)}, u32[]{:S(2)}, u32[]{:S(2)}) %all-to-all-start.3) | async-done | bytes 262176 | tf_op jit(solution)/shard_map/all_to_all | solution.py:21
  530.9 2.4 fusion.8
  533.2 825.0 %all-reduce.2.cloned.1.call-done = f32[2,256,1024]{2,1,0:T(8,128)} async-done(((f32[2,256,1024]{2,1,0:T(8,128)}), f32[2,256,1024]{2,1,0:T(8,128)}) %all-reduce.2.cloned.1.call-update) | async-done | bytes 2097168 | tf_op jit(solution)/shard_map/psum | solution.py:70
  1358.2 1.5 multiply_add_fusion
  (34 shorter events, 3.7 us)
Async XLA Ops:
  7.2 128.5 %all-gather.4.cloned.1.call-start = ((), (), s32[]{:S(2)}) async-start(), calls=%async_computation.6 | async-start | bytes 1064960 | tf_op jit(solution)/shard_map/all_gather | solution.py:30
  8.6 231.8 %all-gather.6.cloned.1.call-start = ((), (), s32[]{:S(2)}) async-start(), calls=%async_computation.7 | async-start | bytes 4718592 | tf_op jit(solution)/shard_map/all_gather | solution.py:38
  135.7 104.7 %copy-start.1 = (bf16[2,256,1024]{2,0,1:T(2,128)(2,1)S(1)}, bf16[2,256,1024]{2,0,1:T(2,128)(2,1)}, u32[]{:S(2)}) copy-start(bf16[2,256,1024]{2,0,1:T(2,128)(2,1)} %all-gather.4.cloned.1.call-done) | copy-start | bytes 3145732
  138.4 153.1 %reduce-scatter.3.cloned.1.call-start = ((), (), s32[]{:S(2)}) async-start(), calls=%async_computation.8 | async-start | bytes 2359296 | tf_op jit(solution)/shard_map/reduce_scatter | solution.py:44
  240.4 3.6 copy-start
  252.3 159.4 %all-gather.8.cloned.1.call-start = ((), (), s32[]{:S(2)}) async-start(), calls=%async_computation.9 | async-start | bytes 2359296 | tf_op jit(solution)/shard_map/all_gather | solution.py:55
  292.6 60.1 %copy-start.3 = (bf16[128,2,256]{2,1,0:T(2,128)(2,1)S(1)}, bf16[128,2,256]{2,1,0:T(2,128)(2,1)}, u32[]{:S(2)}) copy-start(bf16[128,2,256]{2,1,0:T(2,128)(2,1)} %param.6) | copy-start | bytes 393220
  352.7 157.7 %copy-start.2 = (f32[32,8,256]{2,1,0:T(8,128)}, f32[32,8,256]{2,1,0:T(8,128)S(1)}, u32[]{:S(2)}) copy-start(f32[32,8,256]{2,1,0:T(8,128)S(1)} %convert_add_fusion) | copy-start | bytes 786436
  353.5 115.2 %reduce-scatter.5.cloned.1.call-start = ((), (), s32[]{:S(2)}) async-start(), calls=%async_computation.10 | async-start | bytes 2359296 | tf_op jit(solution)/shard_map/reduce_scatter | solution.py:57
  504.2 25.8 %all-to-all-start.3 = ((f32[64,1,1024]{2,1,0:T(1,128)}), f32[64,1,1024]{2,1,0:T(1,128)S(1)}, u32[]{:S(2)}, u32[]{:S(2)}) async-start(f32[64,1,1024]{2,1,0:T(1,128)} %copy.54), calls=%async_computation.5 | async-start | bytes 524288 | tf_op jit(solution)/shard_map/all_to_all | solution.py:21
  510.2 848.1 %all-reduce.2.cloned.1.call-start = ((), (), s32[]{:S(2)}) async-start(), calls=%async_computation.11 | async-start | bytes 4194304 | tf_op jit(solution)/shard_map/psum | solution.py:70
  530.8 827.4 %copy-start.4 = (bf16[2,4,1024]{2,1,0:T(4,128)(2,1)S(1)}, bf16[2,4,1024]{2,1,0:T(4,128)(2,1)}, u32[]{:S(2)}) copy-start(bf16[2,4,1024]{2,1,0:T(4,128)(2,1)} %param.7) | copy-start | bytes 49156
Sparse Core Ops, SparseCore 0:
  10.7 124.9 all-gather.3
  138.6 101.7 all-gather.5
  252.4 39.0 reduce-scatter.2
  353.7 58.0 all-gather.7
  428.5 40.2 reduce-scatter.4
  533.4 824.8 all-reduce.1
where the time goes:
time: 1370 us
  waiting for transfers between devices  1210 us (88%)
  blocking collectives  91.1 us (7%)
  matrix products  34.9 us (3%)
  between operations  14.3 us (1%)
    psum x1, waiting for transfers between devices, per_device(): summed = lax.psum(partial_value, ('row', 'col'))  825 us
    all_gather x1, waiting for transfers between devices, per_device(): full_b = lax.all_gather(factor_b, ('row', 'col'), axis=1, tiled=True)  126 us
    all_gather x1, waiting for transfers between devices, per_device(): lax.all_gather(diff_one, 'row', axis=0, tiled=True)  102 us
    all_to_all x2, blocking collectives, transpose_full(): lax.all_to_all(flat, ('row', 'col'), split_axis=0, concat_axis=0, tiled=T...  65.6 us
    all_gather x1, waiting for transfers between devices, per_device(): lax.all_gather(new_a.reshape(row_count, 2 * R), 'row', axis=0, tiled=True)  58.1 us
    reduce_scatter x1, waiting for transfers between devices, per_device(): lax.psum_scatter(jnp.dot(cov_rows, a_panel, precision=highest, preferred_...  40.4 us
    reduce_scatter x1, waiting for transfers between devices, per_device(): lax.psum_scatter(jnp.dot(cov_rows, panel_flat, precision=highest, preferr...  39.2 us
  transfers between devices with their start and end apart: 7, of which 7 were waited for; matrix products, arithmetic and copies ran while one was open for 0% of the time, Pallas kernels for 0%

commit v1 on v0

--- a/solution.py
+++ b/solution.py
@@ -1,3 +1,4 @@
+import functools
 import jax
 import jax.numpy as jnp
 from jax import lax
@@ -6,6 +7,13 @@
 D = 8192
 O = 1024
 R = 256
+
+
+def expand_the_screen(vals, lane_axis, axis_tag):
+    return jax.lax.psum(jax.lax.psum(vals, lane_axis), axis_tag)
+
+
+set_the_outputs = functools.partial(expand_the_screen, lane_axis="row", axis_tag="col")
 
 
 def reorder_slots(spread):
@@ -67,7 +75,7 @@
         diff_two.astype(jnp.float32),
         precision=highest,
     )
-    summed = lax.psum(partial_value, ("row", "col"))
+    summed = set_the_outputs(partial_value)
     share_rows = factor_b.shape[1]
     linear_id = lax.axis_index("row") * lax.axis_size("col") + lax.axis_index("col")
     own_share = lax.dynamic_slice_in_dim(summed, linear_id * share_rows, share_rows, 1)

time: 1370 us -> 753 us (0.55)
  waiting for transfers between devices: 1210 us -> 593 us
    psum x1 -> x2, waiting for transfers between devices: 825 us -> 210 us  [expand_the_screen(): return jax.lax.psum(jax.lax.psum(vals, lane_axis), axis_tag)]
  transfers between devices with their start and end apart: 7 -> 8, of which waited for: 7 -> 8; matrix products, arithmetic and copies ran while one was open for 0% -> 0% of each run, Pallas kernels for 0% -> 0%
where the time goes in v1:
time: 753 us; the launch traced here: 751 us
  waiting for transfers between devices  593 us (79%)
  blocking collectives  91.1 us (12%)
  matrix products  34.9 us (5%)
  between operations  14.3 us (2%)
  local copies, waits for them, and re-layouts  8.4 us (1%)
    psum x2, waiting for transfers between devices, expand_the_screen(): return jax.lax.psum(jax.lax.psum(vals, lane_axis), axis_tag)  210 us
    all_gather x1, waiting for transfers between devices, per_device(): full_b = lax.all_gather(factor_b, ('row', 'col'), axis=1, tiled=True)  126 us
    all_gather x1, waiting for transfers between devices, per_device(): lax.all_gather(diff_one, 'row', axis=0, tiled=True)  102 us
    all_to_all x2, blocking collectives, transpose_full(): lax.all_to_all(flat, ('row', 'col'), split_axis=0, concat_axis=0, tiled=T...  65.6 us
    all_gather x1, waiting for transfers between devices, per_device(): lax.all_gather(new_a.reshape(row_count, 2 * R), 'row', axis=0, tiled=True)  58.1 us
    reduce_scatter x1, waiting for transfers between devices, per_device(): lax.psum_scatter(jnp.dot(cov_rows, a_panel, precision=highest, preferred_...  40.4 us
    reduce_scatter x1, waiting for transfers between devices, per_device(): lax.psum_scatter(jnp.dot(cov_rows, panel_flat, precision=highest, preferr...  39.2 us
    all_to_all x1, blocking collectives, transpose_full(): lax.all_to_all(reorder_slots(spread), ('row', 'col'), split_axis=0, conca...  25.6 us
  transfers between devices with their start and end apart: 8, of which 8 were waited for; matrix products, arithmetic and copies ran while one was open for 0% of the time, Pallas kernels for 0%

profile of v1, /device:TPU:1, one launch (start us, length us, event | category | flops | bytes accessed | tf_op | source)
XLA Modules:
  0.0 751.3 jit_solution(3866277768567459594)
XLA Ops:
  7.2 1.3 copy.42
  8.6 1.4 copy.41
  10.0 125.7 %all-gather.4.cloned.1.call-done = bf16[2,256,1024]{2,0,1:T(2,128)(2,1)} async-done(((bf16[2,4,1024]{2,0,1:T(2,128)(2,1)}), bf16[2,256,1024]{2,0,1:T(2,128)(2,1)}) %all-gather.4.cloned.1.call-update) | async-done | bytes 1048592 | tf_op jit(solution)/shard_map/all_gather | solution.py:38
  135.7 2.7 fusion.3
  138.5 101.9 %all-gather.6.cloned.1.call-done = bf16[1024,2,1024]{0,2,1:T(8,128)(2,1)} async-done(((bf16[128,2,1024]{0,2,1:T(8,128)(2,1)}), bf16[1024,2,1024]{0,2,1:T(8,128)(2,1)}) %all-gather.6.cloned.1.call-update) | async-done | bytes 4194320 | tf_op jit(solution)/shard_map/all_gather | solution.py:46
  240.4 3.6 fusion.5
  244.0 8.3 %convolution_bitcast_fusion.1 = f32[1024,512]{0,1:T(8,128)} fusion(f32[1024,512]{0,1:T(8,128)S(1)} %bitcast.46, f32[1024,1024]{1,0:T(8,128)S(1)} %copy-done), kind=kOutput, calls=%fused_computation.1 | convolution fusion | flops 6442450944 | bytes 8388608 | tf_op jit(solution)/shard_map/dot_general | solution.py:53
  252.3 39.2 %reduce-scatter.3.cloned.1.call-done = f32[128,512]{0,1:T(8,128)} async-done(((f32[1024,512]{0,1:T(8,128)}), f32[128,512]{0,1:T(8,128)}) %reduce-scatter.3.cloned.1.call-update) | async-done | bytes 262160 | tf_op jit(solution)/shard_map/reduce_scatter | solution.py:52
  291.5 1.1 copy.47
  292.9 32.7 %all_to_all.38 = f32[64,1,1024]{2,1,0:T(1,128)S(1)} all-to-all(f32[64,1,1024]{2,1,0:T(1,128)S(1)} %all_to_all.32), channel_id=1, replica_groups=mesh['layer'=8,'row'=8,'col'=8] {'row','col'}, dimensions={0} | all-to-all | bytes 524288 | tf_op jit(solution)/shard_map/all_to_all | solution.py:28
  326.1 25.6 %all_to_all.39 = f32[64,1,1024]{2,1,0:T(1,128)S(1)} all-to-all(f32[64,1,1024]{2,1,0:T(1,128)S(1)} %copy.50), channel_id=1, replica_groups=mesh['layer'=8,'row'=8,'col'=8] {'row','col'}, dimensions={0} | all-to-all | bytes 524288 | tf_op jit(solution)/shard_map/all_to_all | solution.py:29
  353.6 58.1 %all-gather.8.cloned.1.call-done = f32[1024,512]{1,0:T(8,128)} async-done(((f32[128,512]{1,0:T(8,128)}), f32[1024,512]{1,0:T(8,128)}) %all-gather.8.cloned.1.call-update) | async-done | bytes 2097168 | tf_op jit(solution)/shard_map/all_gather | solution.py:63
  411.7 16.7 %convolution_bitcast_fusion = f32[1024,512]{0,1:T(8,128)} fusion(f32[1024,512]{1,0:T(8,128)} %all-gather.8.cloned.1.call-done, f32[1024,1024]{1,0:T(8,128)} %param.4), kind=kOutput, calls=%fused_computation | convolution fusion | flops 6442450944 | bytes 8388608 | tf_op jit(solution)/shard_map/dot_general | solution.py:66
  428.4 40.4 %reduce-scatter.5.cloned.1.call-done = f32[128,512]{0,1:T(8,128)} async-done(((f32[1024,512]{0,1:T(8,128)}), f32[128,512]{0,1:T(8,128)}) %reduce-scatter.5.cloned.1.call-update) | async-done | bytes 262160 | tf_op jit(solution)/shard_map/reduce_scatter | solution.py:65
  468.8 1.1 copy.51
  470.2 32.8 %all_to_all.40 = f32[64,1,1024]{2,1,0:T(1,128)S(1)} all-to-all(f32[64,1,1024]{2,1,0:T(1,128)S(1)} %all_to_all.33), channel_id=1, replica_groups=mesh['layer'=8,'row'=8,'col'=8] {'row','col'}, dimensions={0} | all-to-all | bytes 524288 | tf_op jit(solution)/shard_map/all_to_all | solution.py:28
  503.2 1.0 copy.54
  504.2 5.9 all-to-all-start.3
  510.4 1.3 fusion.2
  511.8 18.2 %all-to-all-done.3 = f32[64,1,1024]{2,1,0:T(1,128)S(1)} async-done(((f32[64,1,1024]{2,1,0:T(1,128)}), f32[64,1,1024]{2,1,0:T(1,128)S(1)}, u32[]{:S(2)}, u32[]{:S(2)}) %all-to-all-start.3) | async-done | bytes 262176 | tf_op jit(solution)/shard_map/all_to_all | solution.py:29
  530.8 2.3 fusion.8
  533.3 127.8 %all-reduce.3.cloned.1.call-done = f32[2,256,1024]{2,1,0:T(8,128)} async-done(((f32[2,256,1024]{2,1,0:T(8,128)}), f32[2,256,1024]{2,1,0:T(8,128)}) %all-reduce.3.cloned.1.call-update) | async-done | bytes 2097168 | tf_op jit(solution)/shard_map/psum | solution.py:13
  661.1 81.9 %all-reduce.5.cloned.1.call-done = f32[2,256,1024]{2,1,0:T(8,128)} async-done(((f32[2,256,1024]{2,1,0:T(8,128)}), f32[2,256,1024]{2,1,0:T(8,128)}) %all-reduce.5.cloned.1.call-update) | async-done | bytes 2097168 | tf_op jit(solution)/shard_map/psum | solution.py:13
  743.0 1.5 multiply_add_fusion
  (37 shorter events, 4.5 us)
Async XLA Ops:
  7.2 128.5 %all-gather.4.cloned.1.call-start = ((), (), s32[]{:S(2)}) async-start(), calls=%async_computation.6 | async-start | bytes 1064960 | tf_op jit(solution)/shard_map/all_gather | solution.py:38
  8.6 231.8 %all-gather.6.cloned.1.call-start = ((), (), s32[]{:S(2)}) async-start(), calls=%async_computation.7 | async-start | bytes 4718592 | tf_op jit(solution)/shard_map/all_gather | solution.py:46
  135.7 104.7 %copy-start.1 = (bf16[2,256,1024]{2,0,1:T(2,128)(2,1)S(1)}, bf16[2,256,1024]{2,0,1:T(2,128)(2,1)}, u32[]{:S(2)}) copy-start(bf16[2,256,1024]{2,0,1:T(2,128)(2,1)} %all-gather.4.cloned.1.call-done) | copy-start | bytes 3145732
  138.4 153.1 %reduce-scatter.3.cloned.1.call-start = ((), (), s32[]{:S(2)}) async-start(), calls=%async_computation.8 | async-start | bytes 2359296 | tf_op jit(solution)/shard_map/reduce_scatter | solution.py:52
  240.4 3.6 copy-start
  252.3 159.4 %all-gather.8.cloned.1.call-start = ((), (), s32[]{:S(2)}) async-start(), calls=%async_computation.9 | async-start | bytes 2359296 | tf_op jit(solution)/shard_map/all_gather | solution.py:63
  292.6 60.1 %copy-start.3 = (bf16[128,2,256]{2,1,0:T(2,128)(2,1)S(1)}, bf16[128,2,256]{2,1,0:T(2,128)(2,1)}, u32[]{:S(2)}) copy-start(bf16[128,2,256]{2,1,0:T(2,128)(2,1)} %param.6) | copy-start | bytes 393220
  352.7 157.7 %copy-start.2 = (f32[32,8,256]{2,1,0:T(8,128)}, f32[32,8,256]{2,1,0:T(8,128)S(1)}, u32[]{:S(2)}) copy-start(f32[32,8,256]{2,1,0:T(8,128)S(1)} %convert_add_fusion) | copy-start | bytes 786436
  353.5 115.2 %reduce-scatter.5.cloned.1.call-start = ((), (), s32[]{:S(2)}) async-start(), calls=%async_computation.10 | async-start | bytes 2359296 | tf_op jit(solution)/shard_map/reduce_scatter | solution.py:65
  504.2 25.8 %all-to-all-start.3 = ((f32[64,1,1024]{2,1,0:T(1,128)}), f32[64,1,1024]{2,1,0:T(1,128)S(1)}, u32[]{:S(2)}, u32[]{:S(2)}) async-start(f32[64,1,1024]{2,1,0:T(1,128)} %copy.54), calls=%async_computation.5 | async-start | bytes 524288 | tf_op jit(solution)/shard_map/all_to_all | solution.py:29
  510.2 150.9 %all-reduce.3.cloned.1.call-start = ((), (), s32[]{:S(2)}) async-start(), calls=%async_computation.11 | async-start | bytes 4194304 | tf_op jit(solution)/shard_map/psum | solution.py:13
  533.2 209.8 %copy-start.4 = (bf16[2,4,1024]{2,1,0:T(4,128)(2,1)S(1)}, bf16[2,4,1024]{2,1,0:T(4,128)(2,1)}, u32[]{:S(2)}) copy-start(bf16[2,4,1024]{2,1,0:T(4,128)(2,1)} %param.7) | copy-start | bytes 49156
  533.2 209.8 %all-reduce.5.cloned.1.call-start = ((), (), s32[]{:S(2)}) async-start(), calls=%async_computation.12 | async-start | bytes 4194304 | tf_op jit(solution)/shard_map/psum | solution.py:13
Sparse Core Ops, SparseCore 0:
  10.7 124.9 all-gather.3
  138.6 101.7 all-gather.5
  252.4 39.0 reduce-scatter.2
  353.7 58.0 all-gather.7
  428.5 40.2 reduce-scatter.4
  533.3 127.6 all-reduce.2
  663.4 79.5 all-reduce.4
